TPU v7x, 32 devices: a whole 2x2x4 slice. The times are simulated.
32 devices in a mesh: groups: 2 (over y), age: 4 (over z), span: 2 (over x), blade: 2 (over core).
Axes of the slice: x: 2, y: 2, z: 4, core: 2. Of those that a mesh axis runs over, the one named last changes fastest.
Arguments:
- surface_mu: float32 [32, 4, 64, 128], P(('groups', 'age'), 'blade', None, 'span'), parts along dimension 0, may hold values from -6 to 6
- centroid_body: float32 [3, 4, 64, 128], P(None, 'blade', None, 'span'), may hold values from -0.04 to 1.01
- area_normal: float32 [3, 4, 64, 128], P(None, 'blade', None, 'span'), may hold values from -0.12 to 0.12
- te_body: float32 [3, 4, 128], P(None, 'blade', 'span'), may hold values from -0.04 to 1.01
- wake_state: float32 [4, 4, 64, 2, 128], P(None, 'blade', ('groups', 'age'), 'span'), parts along dimension 2, may hold values from -2 to 2
- pairs: int32 [4, 64, 2, 8], P('blade', ('groups', 'age'), 'span'), parts along dimension 1, may hold values from -1 to 71, as said below
- az_index: int32 [6], P('groups'), parts along dimension 0, may hold values from 0 to 15
- free_stream: float32 [6], P('groups'), parts along dimension 0, may hold values from -3 to 3
Outputs:
- wake_final: float32 [4, 4, 64, 2, 128], P(None, 'blade', ('groups', 'age'), 'span'), parts along dimension 2
- wake_velocity: float32 [3, 4, 64, 2, 128], P(None, 'blade', ('groups', 'age'), 'span'), parts along dimension 2
There are 2 independent parts, one for each index of `groups`. A program takes and returns all parts, laid end to end along the dimension named above; an argument that names none is the same for every part. Nothing has to cross between parts.
Inputs may be any that keep to these rules, and one draw needn't show every extreme that they name: Rows come in age blocks of 16 rows (8 tiles), spanwise panels in strips of 64. An entry v >= 0 of pairs[b, t, s, :] names tile v % 8 of age block t // 8 + v // 24 - 1 in strip s + (v // 8) % 3 - 1 of the same blade; -1 marks an empty slot. In each aligned block of 2 blades, one age block and one strip, at most 64 entries are not -1, and exactly 64 in one such block.
All inputs are finite; a program needn't handle non-finite values.
Results may differ from a plain program's by a relative error of at most 0.0003.
Values sent between devices are 32-bit elements; how exact they have to be, the bound alone decides.
A program may use at most 64 MiB of HBM per device.

v0:
```python
import math
import jax
import jax.numpy as jnp
from jax import lax
from jax.sharding import PartitionSpec as P

CB = 8
time_step = 0.05
near_core = 0.0025
far_core = 0.01
inv_four_pi = 0.25 / math.pi


def spread(shard, axis, root):
    mine = lax.axis_index(axis) == root
    return lax.psum(jnp.where(mine, shard, jnp.zeros_like(shard)), axis)


def with_halo(cells, sides, width):
    for axis, dim in sides:
        count = lax.axis_size(axis)
        ends = count - 1
        head = lax.slice_in_dim(cells, 0, width, axis=dim)
        tail = lax.slice_in_dim(cells, cells.shape[dim] - width, cells.shape[dim], axis=dim)
        cells = jnp.concatenate(
            [
                lax.ppermute(tail, axis, [(i, (i + 1) % count) for i in range(ends)]),
                cells,
                lax.ppermute(head, axis, [((i + 1) % count, i) for i in range(ends)]),
            ],
            axis=dim,
        )
    return cells


def shifted(value, axis, steps):
    count = lax.axis_size(axis)
    first, last = (max(0, -steps), min(count, count - steps))
    return lax.ppermute(value, axis, [(source, source + steps) for source in range(first, last)])


def rotate(vector, cosine, sine_val):
    return jnp.stack(
        [
            vector[0] * cosine - vector[1] * sine_val,
            vector[0] * sine_val + vector[1] * cosine,
            vector[2],
        ]
    )


def coarse_sum(values, block_size):
    shape = values.shape
    grouped = values.reshape(
        shape[:-2] + (shape[-2] // block_size, block_size, shape[-1] // block_size, block_size)
    )
    return jnp.sum(grouped, axis=(-3, -1))


def far_velocity(targets, centers, moments):
    separation = targets[:, :, None] - centers[:, None, :]
    dist_sq = jnp.sum(separation * separation, axis=0) + far_core
    inverse = 1.0 / jnp.sqrt(dist_sq)
    inverse_cube = inverse * inverse * inverse
    projection = jnp.sum(moments[:, None, :] * separation, axis=0)
    values = (
        3.0 * projection * inverse_cube * inverse * inverse * separation
        - moments[:, None, :] * inverse_cube
    )
    return inv_four_pi * jnp.sum(values, axis=2)


def near_velocity(targets, sources, strengths):
    separation = targets[:, :, None] - sources[:, None, :]
    dist_sq = jnp.sum(separation * separation, axis=0) + near_core
    weight = 1.0 / (dist_sq * jnp.sqrt(dist_sq))
    cross_prod = jnp.stack(
        [
            strengths[1][None, :] * separation[2] - strengths[2][None, :] * separation[1],
            strengths[2][None, :] * separation[0] - strengths[0][None, :] * separation[2],
            strengths[0][None, :] * separation[1] - strengths[1][None, :] * separation[0],
        ]
    )
    return inv_four_pi * jnp.sum(cross_prod * weight[None], axis=2)


def sheet_strength(pos_pad, mu_pad):
    pos_r = 0.5 * (pos_pad[:, :, 2:, 1:-1] - pos_pad[:, :, :-2, 1:-1])
    pos_s = 0.5 * (pos_pad[:, :, 1:-1, 2:] - pos_pad[:, :, 1:-1, :-2])
    mu_r = 0.5 * (mu_pad[:, 2:, 1:-1] - mu_pad[:, :-2, 1:-1])
    mu_s = 0.5 * (mu_pad[:, 1:-1, 2:] - mu_pad[:, 1:-1, :-2])
    return mu_s[None] * pos_r - mu_r[None] * pos_s


def grouped_map(kernel, operands):
    length = jax.tree.leaves(operands)[0].shape[0]
    turn_count = math.gcd(length, 16)
    shaped = jax.tree.map(
        lambda array: array.reshape((turn_count, length // turn_count) + array.shape[1:]), operands
    )
    result = lax.map(jax.vmap(kernel), shaped)
    return result.reshape((length,) + result.shape[2:])


def far_kernel(centers, moments):

    def apply_one(target_tile):
        return far_velocity(target_tile, centers, moments)

    return apply_one


def near_kernel(bundle):
    return near_velocity(bundle[0], bundle[1], bundle[2])


def on_device(
    surface_mu, centroid_body, area_normal, te_body, wake_state, pairs, az_index, free_stream
):
    az_dev, blade_group, chord_len, span_dev = surface_mu.shape
    tile_dev = wake_state.shape[2]
    lanes = wake_state.shape[4]
    rows_dev = tile_dev * lanes // span_dev
    slot_tile = pairs.shape[3]
    step_count = az_index.shape[0]
    age_count = lax.axis_size("age")
    span_count = lax.axis_size("span")
    blade_count = lax.axis_size("blade")
    age_pos = lax.axis_index("age")
    span_pos = lax.axis_index("span")
    blade_pos = lax.axis_index("blade")
    naz_total = az_dev * age_count
    blade_total = blade_group * blade_count
    tile_local = blade_group * tile_dev
    block_cells = chord_len // CB * (span_dev // CB)
    per_device = blade_group * block_cells
    column = jnp.arange(per_device * span_count * blade_count, dtype=jnp.int32)
    column_blade = (
        column // per_device % blade_count * blade_group + column % per_device // block_cells
    )
    column_frac = column_blade.astype(jnp.float32) / blade_total
    local_frac = (blade_pos * blade_group + jnp.arange(blade_group, dtype=jnp.int32)).astype(
        jnp.float32
    ) / blade_total
    center_local = (coarse_sum(centroid_body, CB) / (CB * CB)).reshape(3, per_device)
    center_all = lax.all_gather(center_local, ("span", "blade"), axis=1, tiled=True)
    sheet_grid = wake_state[:, :, :, 0, :].reshape(4, blade_group, rows_dev, span_dev)
    velocity = jnp.zeros((3, blade_group, tile_dev, lanes), jnp.float32)
    for step_num in range(step_count):
        azimuth = az_index[step_num]
        mu_now = lax.dynamic_index_in_dim(surface_mu, azimuth % az_dev, 0, keepdims=False)
        moment_local = coarse_sum(mu_now[None] * area_normal, CB).reshape(3, per_device)
        trailing_local = (mu_now[:, chord_len - 1, :] - mu_now[:, 0, :]).reshape(
            blade_group * span_dev
        )
        moment_local, trailing_local = (moment_local, trailing_local)
        moment_got, trailing = (
            spread(moment_local, "age", azimuth // az_dev),
            spread(trailing_local, "age", azimuth // az_dev),
        )
        moment_all = lax.all_gather(moment_got, ("span", "blade"), axis=1, tiled=True)
        turn_frac = azimuth.astype(jnp.float32) / naz_total
        source_angle = 2.0 * math.pi * (turn_frac + column_frac)
        source_cos = jnp.cos(source_angle)
        source_sin = jnp.sin(source_angle)
        centers = rotate(center_all, source_cos, source_sin)
        moments = rotate(moment_all, source_cos, source_sin)
        padded = with_halo(sheet_grid, (("age", 2), ("span", 3)), 1)
        pos_pad = padded[:3]
        top_rows = jnp.where(age_pos == 0, pos_pad[:, :, 1, :], pos_pad[:, :, 0, :])
        bottom_rows = jnp.where(
            age_pos == age_count - 1, pos_pad[:, :, -2, :], pos_pad[:, :, -1, :]
        )
        pos_pad = jnp.concatenate(
            [top_rows[:, :, None], pos_pad[:, :, 1:-1], bottom_rows[:, :, None]], 2
        )
        left_cols = jnp.where(span_pos == 0, pos_pad[..., 1], pos_pad[..., 0])
        right_cols = jnp.where(span_pos == span_count - 1, pos_pad[..., -2], pos_pad[..., -1])
        pos_pad = jnp.concatenate(
            [left_cols[..., None], pos_pad[..., 1:-1], right_cols[..., None]], 3
        )
        strength = sheet_strength(pos_pad, padded[3])
        pos_tiles = sheet_grid[:3].reshape(3, blade_group, tile_dev, lanes)
        str_tiles = strength.reshape(3, blade_group, tile_dev, lanes)
        targets = pos_tiles.reshape(3, tile_local, lanes).transpose(1, 0, 2)
        far_field = grouped_map(far_kernel(centers, moments), targets)
        blocks = jnp.concatenate([pos_tiles, str_tiles], 0).transpose(1, 2, 0, 3)[:, None, None]
        beside_all = with_halo(blocks, (("age", 1), ("span", 2)), 1)
        source_table = beside_all.reshape(blade_group, 9 * tile_dev, 6, lanes)
        pair_ids = pairs[:, :, 0, :]
        live_mask = pair_ids >= 0
        safe_ids = jnp.maximum(pair_ids, 0)
        picked = source_table[jnp.arange(blade_group, dtype=jnp.int32)[:, None, None], safe_ids]
        weights = live_mask.astype(jnp.float32)[:, :, :, None, None]
        sources = (
            picked[:, :, :, :3]
            .reshape(tile_local, slot_tile, 3, lanes)
            .transpose(0, 2, 1, 3)
            .reshape(tile_local, 3, slot_tile * lanes)
        )
        strengths = (
            (picked[:, :, :, 3:] * weights)
            .reshape(tile_local, slot_tile, 3, lanes)
            .transpose(0, 2, 1, 3)
            .reshape(tile_local, 3, slot_tile * lanes)
        )
        near_flat = grouped_map(near_kernel, (targets, sources, strengths))
        far_part = far_field.transpose(1, 0, 2).reshape(3, blade_group, tile_dev, lanes)
        near_part = near_flat.transpose(1, 0, 2).reshape(3, blade_group, tile_dev, lanes)
        velocity = free_stream[:, None, None, None] + far_part + near_part
        moved_pos = sheet_grid[:3] + time_step * velocity.reshape(
            3, blade_group, rows_dev, span_dev
        )
        moved_state = jnp.concatenate([moved_pos, sheet_grid[3:4]], 0)
        incoming = shifted(moved_state[:, :, -1, :], "age", 1)
        blade_angle = 2.0 * math.pi * (turn_frac + local_frac)
        te_pos = rotate(te_body, jnp.cos(blade_angle)[:, None], jnp.sin(blade_angle)[:, None])
        shed_row = jnp.concatenate([te_pos, trailing.reshape(1, blade_group, span_dev)], 0)
        incoming = jnp.where(age_pos == 0, shed_row, incoming)
        sheet_grid = jnp.concatenate([incoming[:, :, None, :], moved_state[:, :, :-1, :]], 2)
    final_tiles = sheet_grid.reshape(4, blade_group, tile_dev, lanes)
    return (final_tiles[:, :, :, None, :], velocity[:, :, :, None, :])


def solution(mesh):
    in_specs = (
        P(("groups", "age"), "blade", None, "span"),
        P(None, "blade", None, "span"),
        P(None, "blade", None, "span"),
        P(None, "blade", "span"),
        P(None, "blade", ("groups", "age"), "span", None),
        P("blade", ("groups", "age"), "span", None),
        P("groups"),
        P("groups"),
    )
    out_specs = (
        P(None, "blade", ("groups", "age"), "span", None),
        P(None, "blade", ("groups", "age"), "span", None),
    )
    return jax.shard_map(
        on_device, mesh=mesh, in_specs=in_specs, out_specs=out_specs, check_vma=False
    )
```

profile of v0, /device:TPU:0, one launch (start us, length us, event | category | flops | bytes accessed | tf_op | source)
XLA Modules:
  0.0 256.7 jit_solution(8771473071030211586)
XLA Ops:
  2.7 4.9 %collective-permute-start = (f32[4,2,1,64]{3,1,2,0:T(2,128)S(1)}, f32[4,2,1,64]{3,1,2,0:T(2,128)S(1)}, u32[]{:S(2)}, u32[]{:S(2)}) collective-permute-start(f32[4,2,1,64]{3,1,2,0:T(2,128)S(1)} %copy.303), channel_id=1, source_target_pairs={{0,4},{4,8},{8,12},{1,5},{5,9},{9,13},{2,6},{6,10},{10,14},{3,7},{... | collective-permute-start | bytes 6152 | tf_op jit(solution)/shard_map/ppermute | solution.py:27
  26.2 13.3 %all-reduce = (f32[3,128]{1,0:T(4,128)S(1)}, f32[1,2,64]{2,1,0:T(2,128)S(1)}, f32[3,128]{1,0:T(4,128)S(1)}, f32[1,2,64]{2,1,0:T(2,128)S(1)}, f32[3,128]{1,0:T(4,128)S(1)}, /*index=5*/f32[1,2,64]{2,1,0:T(2,128)S(1)}) all-reduce(f32[3,128]{1,0:T(4,128)S(1)} %select_n.377, ...), channel_id=1, replica_groups=mesh['groups'=2,'age'=4,'span'=2,'blade'=2] {'age'}, use_global_device_ids=true, to_apply=%region_5.6 | all-reduce | flops 1536 | bytes 12288 | tf_op jit(solution)/shard_map/psum | solution.py:16
  39.6 5.2 %all_gather.12 = f32[3,512]{1,0:T(4,128)S(1)} all-gather(f32[3,128]{1,0:T(4,128)S(1)} %get-tuple-element.344), channel_id=1, replica_groups=mesh['groups'=2,'age'=4,'span'=2,'blade'=2] {'span','blade'}, dimensions={1}, use_global_device_ids=true | all-gather | bytes 7680 | tf_op jit(solution)/shard_map/all_gather | solution.py:161
  45.5 5.2 %all_gather.13 = f32[3,512]{1,0:T(4,128)S(1)} all-gather(f32[3,128]{1,0:T(4,128)S(1)} %div.142), channel_id=1, replica_groups=mesh['groups'=2,'age'=4,'span'=2,'blade'=2] {'span','blade'}, dimensions={1}, use_global_device_ids=true | all-gather | bytes 7680 | tf_op jit(solution)/shard_map/all_gather | solution.py:146
  51.0 9.9 %while.60 = (s32[]{:T(128)}, f32[16,1,3,128]{3,2,1,0:T(4,128)S(1)}, f32[3,512]{1,0:T(4,128)S(1)}, f32[16,1,3,128]{3,2,1,0:T(4,128)S(1)}, f32[3,512]{1,0:T(4,128)S(1)}, /*index=5*/s32[]{:T(128)}) while((s32[]{:T(128)}, f32[16,1,3,128]{3,2,1,0:T(4,128)S(1)}, f32[3,512]{1,0:T(4,128)S(1)}, f32[16,1,3,128]{3,2,1,0:T(4,128)S(1)}, ...), condition=%wide.region_10.11_spmd, body=%wide.region_6.10_spmd.sunk | while | flops 2293762 | bytes 2133589 | solution.py:101
  60.9 5.2 %all_gather.14 = f32[3,512]{1,0:T(4,128)S(1)} all-gather(f32[3,128]{1,0:T(4,128)S(1)} %get-tuple-element.346), channel_id=1, replica_groups=mesh['groups'=2,'age'=4,'span'=2,'blade'=2] {'span','blade'}, dimensions={1}, use_global_device_ids=true | all-gather | bytes 7680 | tf_op jit(solution)/shard_map/all_gather | solution.py:161
  68.5 4.5 %collective-permute-start.2 = (f32[4,2,18,1]{3,1,2,0:T(2,128)S(1)}, f32[4,2,18,1]{3,1,2,0:T(2,128)S(1)}, u32[]{:S(2)}, u32[]{:S(2)}) collective-permute-start(f32[4,2,18,1]{3,1,2,0:T(2,128)S(1)} %get-tuple-element.398), channel_id=1, source_target_pairs={{0,2},{1,3},{4,6},{5,7},{8,10},{9,11},{12,14},{13,15},{16,18},{17,... | collective-permute-start | bytes 1736 | tf_op jit(solution)/shard_map/ppermute | solution.py:27
  77.7 4.5 %collective-permute-start.4 = (f32[2,1,1,8,6,128]{5,3,0,4,2,1:T(8,128)S(1)}, f32[2,1,1,8,6,128]{5,3,0,4,2,1:T(8,128)S(1)}, u32[]{:S(2)}, u32[]{:S(2)}) collective-permute-start(f32[2,1,1,8,6,128]{5,3,0,4,2,1:T(8,128)S(1)} %maximum_bitcast_fusion.3), channel_id=1, source_target_pairs={{0,4},{4,8},{8,12},{1,5},{5,9},{9,13},{2,6},{6,10},{10,14},{3,7},{... | collective-permute-start | bytes 147464 | tf_op jit(solution)/shard_map/ppermute | solution.py:27
  85.3 4.6 %collective-permute-start.6 = (f32[2,3,1,8,6,128]{5,3,0,4,2,1:T(8,128)S(1)}, f32[2,3,1,8,6,128]{5,3,0,4,2,1:T(8,128)S(1)}, u32[]{:S(2)}, u32[]{:S(2)}) collective-permute-start(f32[2,3,1,8,6,128]{5,3,0,4,2,1:T(8,128)S(1)} %pad_maximum_fusion.3), channel_id=1, source_target_pairs={{0,2},{1,3},{4,6},{5,7},{8,10},{9,11},{12,14},{13,15},{16,18},{17,... | collective-permute-start | bytes 442376 | tf_op jit(solution)/shard_map/ppermute | solution.py:27
  94.0 19.9 %while.61 = (s32[]{:T(128)}, f32[16,1,3,128]{3,2,1,0:T(4,128)S(1)}, f32[16,1,3,1024]{3,0,2,1:T(8,128)S(1)}, f32[16,1,3,128]{3,2,1,0:T(4,128)S(1)}, f32[16,1,3,1024]{3,0,2,1:T(8,128)S(1)}, /*index=5*/s32[]{:T(128)}) while((s32[]{:T(128)}, f32[16,1,3,128]{3,2,1,0:T(4,128)S(1)}, f32[16,1,3,1024]{3,0,2,1:T(8,128)S(1)}, ...), condition=%wide.region_14.15_spmd, body=%wide.region_11.14_spmd.sunk | while | flops 4587522 | bytes 8560217 | solution.py:101
  114.2 4.2 %collective-permute-start.8 = (f32[4,2,64]{2,1,0:T(2,128)S(1)}, f32[4,2,64]{2,1,0:T(2,128)S(1)}, u32[]{:S(2)}, u32[]{:S(2)}) collective-permute-start(f32[4,2,64]{2,1,0:T(2,128)S(1)} %get-tuple-element.403), channel_id=1, source_target_pairs={{0,4},{4,8},{8,12},{1,5},{5,9},{9,13},{2,6},{6,10},{10,14},{3,7},{... | collective-permute-start | bytes 6152 | tf_op jit(solution)/shard_map/ppermute | solution.py:39
  127.5 4.5 %collective-permute-start.11 = (f32[4,2,18,1]{3,1,0,2:T(2,128)S(1)}, f32[4,2,18,1]{3,1,0,2:T(2,128)S(1)}, u32[]{:S(2)}, u32[]{:S(2)}) collective-permute-start(f32[4,2,18,1]{3,1,0,2:T(2,128)S(1)} %get-tuple-element.396), channel_id=1, source_target_pairs={{0,2},{1,3},{4,6},{5,7},{8,10},{9,11},{12,14},{13,15},{16,18},{17,... | collective-permute-start | bytes 1736 | tf_op jit(solution)/shard_map/ppermute | solution.py:27
  136.7 4.5 %collective-permute-start.13 = (f32[2,1,1,8,6,128]{5,3,0,4,2,1:T(8,128)S(1)}, f32[2,1,1,8,6,128]{5,3,0,4,2,1:T(8,128)S(1)}, u32[]{:S(2)}, u32[]{:S(2)}) collective-permute-start(f32[2,1,1,8,6,128]{5,3,0,4,2,1:T(8,128)S(1)} %maximum_bitcast_fusion.4), channel_id=1, source_target_pairs={{0,4},{4,8},{8,12},{1,5},{5,9},{9,13},{2,6},{6,10},{10,14},{3,7},{... | collective-permute-start | bytes 147464 | tf_op jit(solution)/shard_map/ppermute | solution.py:27
  141.3 5.5 %all_gather.15 = f32[3,512]{1,0:T(4,128)S(1)} all-gather(f32[3,128]{1,0:T(4,128)S(1)} %get-tuple-element.348), channel_id=1, replica_groups=mesh['groups'=2,'age'=4,'span'=2,'blade'=2] {'span','blade'}, dimensions={1}, use_global_device_ids=true | all-gather | bytes 7680 | tf_op jit(solution)/shard_map/all_gather | solution.py:161
  148.3 4.7 %collective-permute-start.15 = (f32[2,3,1,8,6,128]{5,3,0,4,2,1:T(8,128)S(1)}, f32[2,3,1,8,6,128]{5,3,0,4,2,1:T(8,128)S(1)}, u32[]{:S(2)}, u32[]{:S(2)}) collective-permute-start(f32[2,3,1,8,6,128]{5,3,0,4,2,1:T(8,128)S(1)} %pad_maximum_fusion.4), channel_id=1, source_target_pairs={{0,2},{1,3},{4,6},{5,7},{8,10},{9,11},{12,14},{13,15},{16,18},{17,... | collective-permute-start | bytes 442376 | tf_op jit(solution)/shard_map/ppermute | solution.py:27
  153.1 9.9 %while.62 = (s32[]{:T(128)}, f32[16,1,3,128]{3,2,1,0:T(4,128)S(1)}, f32[3,512]{1,0:T(4,128)S(1)}, f32[16,1,3,128]{3,2,1,0:T(4,128)S(1)}, f32[3,512]{1,0:T(4,128)S(1)}, /*index=5*/s32[]{:T(128)}) while((s32[]{:T(128)}, f32[16,1,3,128]{3,2,1,0:T(4,128)S(1)}, f32[3,512]{1,0:T(4,128)S(1)}, f32[16,1,3,128]{3,2,1,0:T(4,128)S(1)}, ...), condition=%wide.region_21.22_spmd, body=%wide.region_17.21_spmd.sunk | while | flops 2293762 | bytes 2133589 | solution.py:101
  164.6 19.9 %while.63 = (s32[]{:T(128)}, f32[16,1,3,128]{3,2,1,0:T(4,128)S(1)}, f32[16,1,3,1024]{3,0,2,1:T(8,128)S(1)}, f32[16,1,3,128]{3,2,1,0:T(4,128)S(1)}, f32[16,1,3,1024]{3,0,2,1:T(8,128)S(1)}, /*index=5*/s32[]{:T(128)}) while((s32[]{:T(128)}, f32[16,1,3,128]{3,2,1,0:T(4,128)S(1)}, f32[16,1,3,1024]{3,0,2,1:T(8,128)S(1)}, ...), condition=%wide.region_25.26_spmd, body=%wide.region_22.25_spmd.sunk | while | flops 4587522 | bytes 8560217 | solution.py:101
  191.6 4.2 %collective-permute-done.19 = f32[4,2,1,64]{3,1,2,0:T(2,128)S(1)} collective-permute-done((f32[4,2,1,64]{3,1,2,0:T(2,128)S(1)}, f32[4,2,1,64]{3,1,2,0:T(2,128)S(1)}, u32[]{:S(2)}, u32[]{:S(2)}) %collective-permute-start.19) | collective-permute-done | bytes 2080 | tf_op jit(solution)/shard_map/ppermute | solution.py:29
  197.3 4.5 %collective-permute-start.20 = (f32[4,2,18,1]{3,1,2,0:T(2,128)S(1)}, f32[4,2,18,1]{3,1,2,0:T(2,128)S(1)}, u32[]{:S(2)}, u32[]{:S(2)}) collective-permute-start(f32[4,2,18,1]{3,1,2,0:T(2,128)S(1)} %get-tuple-element.394), channel_id=1, source_target_pairs={{0,2},{1,3},{4,6},{5,7},{8,10},{9,11},{12,14},{13,15},{16,18},{17,... | collective-permute-start | bytes 1736 | tf_op jit(solution)/shard_map/ppermute | solution.py:27
  206.6 4.5 %collective-permute-start.22 = (f32[2,1,1,8,6,128]{5,3,0,4,2,1:T(8,128)S(1)}, f32[2,1,1,8,6,128]{5,3,0,4,2,1:T(8,128)S(1)}, u32[]{:S(2)}, u32[]{:S(2)}) collective-permute-start(f32[2,1,1,8,6,128]{5,3,0,4,2,1:T(8,128)S(1)} %maximum_bitcast_fusion.5), channel_id=1, source_target_pairs={{0,4},{4,8},{8,12},{1,5},{5,9},{9,13},{2,6},{6,10},{10,14},{3,7},{... | collective-permute-start | bytes 147464 | tf_op jit(solution)/shard_map/ppermute | solution.py:27
  214.2 4.6 %collective-permute-start.24 = (f32[2,3,1,8,6,128]{5,3,0,4,2,1:T(8,128)S(1)}, f32[2,3,1,8,6,128]{5,3,0,4,2,1:T(8,128)S(1)}, u32[]{:S(2)}, u32[]{:S(2)}) collective-permute-start(f32[2,3,1,8,6,128]{5,3,0,4,2,1:T(8,128)S(1)} %pad_maximum_fusion.5), channel_id=1, source_target_pairs={{0,2},{1,3},{4,6},{5,7},{8,10},{9,11},{12,14},{13,15},{16,18},{17,... | collective-permute-start | bytes 442376 | tf_op jit(solution)/shard_map/ppermute | solution.py:27
  218.8 9.9 %while.64 = (s32[]{:T(128)}, f32[16,1,3,128]{3,2,1,0:T(4,128)S(1)}, f32[3,512]{1,0:T(4,128)S(1)}, f32[16,1,3,128]{3,2,1,0:T(4,128)S(1)}, f32[3,512]{1,0:T(4,128)S(1)}, /*index=5*/s32[]{:T(128)}) while((s32[]{:T(128)}, f32[16,1,3,128]{3,2,1,0:T(4,128)S(1)}, f32[3,512]{1,0:T(4,128)S(1)}, f32[16,1,3,128]{3,2,1,0:T(4,128)S(1)}, ...), condition=%wide.region_32.33_spmd, body=%wide.region_28.32_spmd.sunk | while | flops 2293762 | bytes 2133589 | solution.py:101
  230.3 19.9 %while.65 = (s32[]{:T(128)}, f32[16,1,3,128]{3,2,1,0:T(4,128)S(1)}, f32[16,1,3,1024]{3,0,2,1:T(8,128)S(1)}, f32[16,1,3,128]{3,2,1,0:T(4,128)S(1)}, f32[16,1,3,1024]{3,0,2,1:T(8,128)S(1)}, /*index=5*/s32[]{:T(128)}) while((s32[]{:T(128)}, f32[16,1,3,128]{3,2,1,0:T(4,128)S(1)}, f32[16,1,3,1024]{3,0,2,1:T(8,128)S(1)}, ...), condition=%wide.region_36.37_spmd, body=%wide.region_33.36_spmd.sunk | while | flops 4587522 | bytes 8560217 | solution.py:101
  250.4 4.2 %collective-permute-start.26 = (f32[4,2,64]{2,1,0:T(2,128)S(1)}, f32[4,2,64]{2,1,0:T(2,128)S(1)}, u32[]{:S(2)}, u32[]{:S(2)}) collective-permute-start(f32[4,2,64]{2,1,0:T(2,128)S(1)} %bitcast.385), channel_id=1, source_target_pairs={{0,4},{4,8},{8,12},{1,5},{5,9},{9,13},{2,6},{6,10},{10,14},{3,7},{... | collective-permute-start | bytes 6152 | tf_op jit(solution)/shard_map/ppermute | solution.py:39
  (981 shorter events, 146.4 us)
Async XLA Ops:
  2.7 64.2 %collective-permute-start = (f32[4,2,1,64]{3,1,2,0:T(2,128)S(1)}, f32[4,2,1,64]{3,1,2,0:T(2,128)S(1)}, u32[]{:S(2)}, u32[]{:S(2)}) collective-permute-start(f32[4,2,1,64]{3,1,2,0:T(2,128)S(1)} %copy.303), channel_id=1, source_target_pairs={{0,4},{4,8},{8,12},{1,5},{5,9},{9,13},{2,6},{6,10},{10,14},{3,7},{... | collective-permute-start | bytes 6152 | tf_op jit(solution)/shard_map/ppermute | solution.py:27
  7.7 59.3 %collective-permute-start.1 = (f32[4,2,1,64]{3,1,2,0:T(2,128)S(1)}, f32[4,2,1,64]{3,1,2,0:T(2,128)S(1)}, u32[]{:S(2)}, u32[]{:S(2)}) collective-permute-start(f32[4,2,1,64]{3,1,2,0:T(2,128)S(1)} %copy.304), channel_id=1, source_target_pairs={{4,0},{8,4},{12,8},{5,1},{9,5},{13,9},{6,2},{10,6},{14,10},{7,3},{... | collective-permute-start | bytes 6152 | tf_op jit(solution)/shard_map/ppermute | solution.py:29
  67.2 6.4 %collective-permute-start.3 = (f32[4,2,18,1]{3,1,2,0:T(2,128)S(1)}, f32[4,2,18,1]{3,1,2,0:T(2,128)S(1)}, u32[]{:S(2)}, u32[]{:S(2)}) collective-permute-start(f32[4,2,18,1]{3,1,2,0:T(2,128)S(1)} %get-tuple-element.399), channel_id=1, source_target_pairs={{2,0},{3,1},{6,4},{7,5},{10,8},{11,9},{14,12},{15,13},{18,16},{19,... | collective-permute-start | bytes 1736 | tf_op jit(solution)/shard_map/ppermute | solution.py:29
  68.5 6.5 %collective-permute-start.2 = (f32[4,2,18,1]{3,1,2,0:T(2,128)S(1)}, f32[4,2,18,1]{3,1,2,0:T(2,128)S(1)}, u32[]{:S(2)}, u32[]{:S(2)}) collective-permute-start(f32[4,2,18,1]{3,1,2,0:T(2,128)S(1)} %get-tuple-element.398), channel_id=1, source_target_pairs={{0,2},{1,3},{4,6},{5,7},{8,10},{9,11},{12,14},{13,15},{16,18},{17,... | collective-permute-start | bytes 1736 | tf_op jit(solution)/shard_map/ppermute | solution.py:27
  76.4 6.0 %collective-permute-start.5 = (f32[2,1,1,8,6,128]{5,3,0,4,2,1:T(8,128)S(1)}, f32[2,1,1,8,6,128]{5,3,0,4,2,1:T(8,128)S(1)}, u32[]{:S(2)}, u32[]{:S(2)}) collective-permute-start(f32[2,1,1,8,6,128]{5,3,0,4,2,1:T(8,128)S(1)} %maximum_bitcast_fusion.3), channel_id=1, source_target_pairs={{4,0},{8,4},{12,8},{5,1},{9,5},{13,9},{6,2},{10,6},{14,10},{7,3},{... | collective-permute-start | bytes 147464 | tf_op jit(solution)/shard_map/ppermute | solution.py:29
  77.7 6.3 %collective-permute-start.4 = (f32[2,1,1,8,6,128]{5,3,0,4,2,1:T(8,128)S(1)}, f32[2,1,1,8,6,128]{5,3,0,4,2,1:T(8,128)S(1)}, u32[]{:S(2)}, u32[]{:S(2)}) collective-permute-start(f32[2,1,1,8,6,128]{5,3,0,4,2,1:T(8,128)S(1)} %maximum_bitcast_fusion.3), channel_id=1, source_target_pairs={{0,4},{4,8},{8,12},{1,5},{5,9},{9,13},{2,6},{6,10},{10,14},{3,7},{... | collective-permute-start | bytes 147464 | tf_op jit(solution)/shard_map/ppermute | solution.py:27
  84.0 7.0 %collective-permute-start.7 = (f32[2,3,1,8,6,128]{5,3,0,4,2,1:T(8,128)S(1)}, f32[2,3,1,8,6,128]{5,3,0,4,2,1:T(8,128)S(1)}, u32[]{:S(2)}, u32[]{:S(2)}) collective-permute-start(f32[2,3,1,8,6,128]{5,3,0,4,2,1:T(8,128)S(1)} %pad_maximum_fusion.3), channel_id=1, source_target_pairs={{2,0},{3,1},{6,4},{7,5},{10,8},{11,9},{14,12},{15,13},{18,16},{19,... | collective-permute-start | bytes 442376 | tf_op jit(solution)/shard_map/ppermute | solution.py:29
  85.3 7.2 %collective-permute-start.6 = (f32[2,3,1,8,6,128]{5,3,0,4,2,1:T(8,128)S(1)}, f32[2,3,1,8,6,128]{5,3,0,4,2,1:T(8,128)S(1)}, u32[]{:S(2)}, u32[]{:S(2)}) collective-permute-start(f32[2,3,1,8,6,128]{5,3,0,4,2,1:T(8,128)S(1)} %pad_maximum_fusion.3), channel_id=1, source_target_pairs={{0,2},{1,3},{4,6},{5,7},{8,10},{9,11},{12,14},{13,15},{16,18},{17,... | collective-permute-start | bytes 442376 | tf_op jit(solution)/shard_map/ppermute | solution.py:27
  114.2 6.3 %collective-permute-start.8 = (f32[4,2,64]{2,1,0:T(2,128)S(1)}, f32[4,2,64]{2,1,0:T(2,128)S(1)}, u32[]{:S(2)}, u32[]{:S(2)}) collective-permute-start(f32[4,2,64]{2,1,0:T(2,128)S(1)} %get-tuple-element.403), channel_id=1, source_target_pairs={{0,4},{4,8},{8,12},{1,5},{5,9},{9,13},{2,6},{6,10},{10,14},{3,7},{... | collective-permute-start | bytes 6152 | tf_op jit(solution)/shard_map/ppermute | solution.py:39
  120.5 5.5 %collective-permute-start.10 = (f32[4,2,1,64]{3,1,0,2:T(2,128)S(1)}, f32[4,2,1,64]{3,1,0,2:T(2,128)S(1)}, u32[]{:S(2)}, u32[]{:S(2)}) collective-permute-start(f32[4,2,1,64]{3,1,0,2:T(2,128)S(1)} %fusion.57), channel_id=1, source_target_pairs={{4,0},{8,4},{12,8},{5,1},{9,5},{13,9},{6,2},{10,6},{14,10},{7,3},{... | collective-permute-start | bytes 6152 | tf_op jit(solution)/shard_map/ppermute | solution.py:29
  126.2 6.2 %collective-permute-start.12 = (f32[4,2,18,1]{3,1,0,2:T(2,128)S(1)}, f32[4,2,18,1]{3,1,0,2:T(2,128)S(1)}, u32[]{:S(2)}, u32[]{:S(2)}) collective-permute-start(f32[4,2,18,1]{3,1,0,2:T(2,128)S(1)} %get-tuple-element.397), channel_id=1, source_target_pairs={{2,0},{3,1},{6,4},{7,5},{10,8},{11,9},{14,12},{15,13},{18,16},{19,... | collective-permute-start | bytes 1736 | tf_op jit(solution)/shard_map/ppermute | solution.py:29
  127.5 6.5 %collective-permute-start.11 = (f32[4,2,18,1]{3,1,0,2:T(2,128)S(1)}, f32[4,2,18,1]{3,1,0,2:T(2,128)S(1)}, u32[]{:S(2)}, u32[]{:S(2)}) collective-permute-start(f32[4,2,18,1]{3,1,0,2:T(2,128)S(1)} %get-tuple-element.396), channel_id=1, source_target_pairs={{0,2},{1,3},{4,6},{5,7},{8,10},{9,11},{12,14},{13,15},{16,18},{17,... | collective-permute-start | bytes 1736 | tf_op jit(solution)/shard_map/ppermute | solution.py:27
  135.4 11.5 %collective-permute-start.14 = (f32[2,1,1,8,6,128]{5,3,0,4,2,1:T(8,128)S(1)}, f32[2,1,1,8,6,128]{5,3,0,4,2,1:T(8,128)S(1)}, u32[]{:S(2)}, u32[]{:S(2)}) collective-permute-start(f32[2,1,1,8,6,128]{5,3,0,4,2,1:T(8,128)S(1)} %maximum_bitcast_fusion.4), channel_id=1, source_target_pairs={{4,0},{8,4},{12,8},{5,1},{9,5},{13,9},{6,2},{10,6},{14,10},{7,3},{... | collective-permute-start | bytes 147464 | tf_op jit(solution)/shard_map/ppermute | solution.py:29
  136.7 10.2 %collective-permute-start.13 = (f32[2,1,1,8,6,128]{5,3,0,4,2,1:T(8,128)S(1)}, f32[2,1,1,8,6,128]{5,3,0,4,2,1:T(8,128)S(1)}, u32[]{:S(2)}, u32[]{:S(2)}) collective-permute-start(f32[2,1,1,8,6,128]{5,3,0,4,2,1:T(8,128)S(1)} %maximum_bitcast_fusion.4), channel_id=1, source_target_pairs={{0,4},{4,8},{8,12},{1,5},{5,9},{9,13},{2,6},{6,10},{10,14},{3,7},{... | collective-permute-start | bytes 147464 | tf_op jit(solution)/shard_map/ppermute | solution.py:27
  147.0 16.1 %collective-permute-start.16 = (f32[2,3,1,8,6,128]{5,3,0,4,2,1:T(8,128)S(1)}, f32[2,3,1,8,6,128]{5,3,0,4,2,1:T(8,128)S(1)}, u32[]{:S(2)}, u32[]{:S(2)}) collective-permute-start(f32[2,3,1,8,6,128]{5,3,0,4,2,1:T(8,128)S(1)} %pad_maximum_fusion.4), channel_id=1, source_target_pairs={{2,0},{3,1},{6,4},{7,5},{10,8},{11,9},{14,12},{15,13},{18,16},{19,... | collective-permute-start | bytes 442376 | tf_op jit(solution)/shard_map/ppermute | solution.py:29
  148.3 14.8 %collective-permute-start.15 = (f32[2,3,1,8,6,128]{5,3,0,4,2,1:T(8,128)S(1)}, f32[2,3,1,8,6,128]{5,3,0,4,2,1:T(8,128)S(1)}, u32[]{:S(2)}, u32[]{:S(2)}) collective-permute-start(f32[2,3,1,8,6,128]{5,3,0,4,2,1:T(8,128)S(1)} %pad_maximum_fusion.4), channel_id=1, source_target_pairs={{0,2},{1,3},{4,6},{5,7},{8,10},{9,11},{12,14},{13,15},{16,18},{17,... | collective-permute-start | bytes 442376 | tf_op jit(solution)/shard_map/ppermute | solution.py:27
  184.8 5.5 %collective-permute-start.17 = (f32[4,2,64]{2,1,0:T(2,128)S(1)}, f32[4,2,64]{2,1,0:T(2,128)S(1)}, u32[]{:S(2)}, u32[]{:S(2)}) collective-permute-start(f32[4,2,64]{2,1,0:T(2,128)S(1)} %get-tuple-element.401), channel_id=1, source_target_pairs={{0,4},{4,8},{8,12},{1,5},{5,9},{9,13},{2,6},{6,10},{10,14},{3,7},{... | collective-permute-start | bytes 6152 | tf_op jit(solution)/shard_map/ppermute | solution.py:39
  196.0 6.2 %collective-permute-start.21 = (f32[4,2,18,1]{3,1,2,0:T(2,128)S(1)}, f32[4,2,18,1]{3,1,2,0:T(2,128)S(1)}, u32[]{:S(2)}, u32[]{:S(2)}) collective-permute-start(f32[4,2,18,1]{3,1,2,0:T(2,128)S(1)} %get-tuple-element.395), channel_id=1, source_target_pairs={{2,0},{3,1},{6,4},{7,5},{10,8},{11,9},{14,12},{15,13},{18,16},{19,... | collective-permute-start | bytes 1736 | tf_op jit(solution)/shard_map/ppermute | solution.py:29
  197.3 6.5 %collective-permute-start.20 = (f32[4,2,18,1]{3,1,2,0:T(2,128)S(1)}, f32[4,2,18,1]{3,1,2,0:T(2,128)S(1)}, u32[]{:S(2)}, u32[]{:S(2)}) collective-permute-start(f32[4,2,18,1]{3,1,2,0:T(2,128)S(1)} %get-tuple-element.394), channel_id=1, source_target_pairs={{0,2},{1,3},{4,6},{5,7},{8,10},{9,11},{12,14},{13,15},{16,18},{17,... | collective-permute-start | bytes 1736 | tf_op jit(solution)/shard_map/ppermute | solution.py:27
  205.3 6.0 %collective-permute-start.23 = (f32[2,1,1,8,6,128]{5,3,0,4,2,1:T(8,128)S(1)}, f32[2,1,1,8,6,128]{5,3,0,4,2,1:T(8,128)S(1)}, u32[]{:S(2)}, u32[]{:S(2)}) collective-permute-start(f32[2,1,1,8,6,128]{5,3,0,4,2,1:T(8,128)S(1)} %maximum_bitcast_fusion.5), channel_id=1, source_target_pairs={{4,0},{8,4},{12,8},{5,1},{9,5},{13,9},{6,2},{10,6},{14,10},{7,3},{... | collective-permute-start | bytes 147464 | tf_op jit(solution)/shard_map/ppermute | solution.py:29
  206.6 6.3 %collective-permute-start.22 = (f32[2,1,1,8,6,128]{5,3,0,4,2,1:T(8,128)S(1)}, f32[2,1,1,8,6,128]{5,3,0,4,2,1:T(8,128)S(1)}, u32[]{:S(2)}, u32[]{:S(2)}) collective-permute-start(f32[2,1,1,8,6,128]{5,3,0,4,2,1:T(8,128)S(1)} %maximum_bitcast_fusion.5), channel_id=1, source_target_pairs={{0,4},{4,8},{8,12},{1,5},{5,9},{9,13},{2,6},{6,10},{10,14},{3,7},{... | collective-permute-start | bytes 147464 | tf_op jit(solution)/shard_map/ppermute | solution.py:27
  212.9 15.9 %collective-permute-start.25 = (f32[2,3,1,8,6,128]{5,3,0,4,2,1:T(8,128)S(1)}, f32[2,3,1,8,6,128]{5,3,0,4,2,1:T(8,128)S(1)}, u32[]{:S(2)}, u32[]{:S(2)}) collective-permute-start(f32[2,3,1,8,6,128]{5,3,0,4,2,1:T(8,128)S(1)} %pad_maximum_fusion.5), channel_id=1, source_target_pairs={{2,0},{3,1},{6,4},{7,5},{10,8},{11,9},{14,12},{15,13},{18,16},{19,... | collective-permute-start | bytes 442376 | tf_op jit(solution)/shard_map/ppermute | solution.py:29
  214.2 14.6 %collective-permute-start.24 = (f32[2,3,1,8,6,128]{5,3,0,4,2,1:T(8,128)S(1)}, f32[2,3,1,8,6,128]{5,3,0,4,2,1:T(8,128)S(1)}, u32[]{:S(2)}, u32[]{:S(2)}) collective-permute-start(f32[2,3,1,8,6,128]{5,3,0,4,2,1:T(8,128)S(1)} %pad_maximum_fusion.5), channel_id=1, source_target_pairs={{0,2},{1,3},{4,6},{5,7},{8,10},{9,11},{12,14},{13,15},{16,18},{17,... | collective-permute-start | bytes 442376 | tf_op jit(solution)/shard_map/ppermute | solution.py:27
  250.4 5.6 %collective-permute-start.26 = (f32[4,2,64]{2,1,0:T(2,128)S(1)}, f32[4,2,64]{2,1,0:T(2,128)S(1)}, u32[]{:S(2)}, u32[]{:S(2)}) collective-permute-start(f32[4,2,64]{2,1,0:T(2,128)S(1)} %bitcast.385), channel_id=1, source_target_pairs={{0,4},{4,8},{8,12},{1,5},{5,9},{9,13},{2,6},{6,10},{10,14},{3,7},{... | collective-permute-start | bytes 6152 | tf_op jit(solution)/shard_map/ppermute | solution.py:39
  (6 other events, 75.8 us)
where the time goes:
time: 258 us; the launch traced here: 257 us
  other arithmetic  91.1 us (35%)
  starting transfers between devices  77.3 us (30%)
  blocking collectives  34.4 us (13%)
  waiting for transfers between devices  20.1 us (8%)
  local copies, waits for them, and re-layouts  16.5 us (6%)
  between operations  11.3 us (4%)
  loops' own time  5.87 us (2%)
    ppermute x12, starting transfers between devices, with_halo(): lax.ppermute(tail, axis, [(i, (i + 1) % count) for i in range(ends)])  49.9 us
    all_gather x3, blocking collectives, on_device(): lax.all_gather(moment_got, ('span', 'blade'), axis=1, tiled=True)  15.9 us
    ppermute x12, starting transfers between devices, with_halo(): lax.ppermute(head, axis, [((i + 1) % count, i) for i in range(ends)])  15.5 us
    sub x48, other arithmetic, near_velocity(): strengths[1][None, :] * separation[2]  14.4 us
    reduce_sum x48, other arithmetic, far_velocity(): return inv_four_pi * jnp.sum(values, axis=2)  13.4 us
    psum x1, blocking collectives, spread(): return lax.psum(jnp.where(mine, shard, jnp.zeros_like(shard)), axis)  13.3 us
    ppermute x3, starting transfers between devices, shifted(): lax.ppermute(value, axis, [(source, source + steps) for source in range(f...  11.9 us
    reduce_sum x48, other arithmetic, near_velocity(): dist_sq = jnp.sum(separation * separation, axis=0) + near_core  10.6 us
  transfers between devices with their start and end apart: 27, of which 14 were waited for; matrix products, arithmetic and copies ran while one was open for 15% of the time, Pallas kernels for 0%

commit v1 on v0

--- a/solution.py
+++ b/solution.py
@@ -158,7 +158,18 @@
             spread(moment_local, "age", azimuth // az_dev),
             spread(trailing_local, "age", azimuth // az_dev),
         )
-        moment_all = lax.all_gather(moment_got, ("span", "blade"), axis=1, tiled=True)
+        ways = lax.axis_size(("span", "blade"))
+        up = [(d, (d + 1) % ways) for d in range(ways)]
+        down = [(d, (d - 1) % ways) for d in range(ways)]
+        earlier, later = ([moment_got], [moment_got])
+        for _ in range(ways // 2):
+            earlier.append(lax.ppermute(earlier[-1], ("span", "blade"), up))
+        for _ in range((ways - 1) // 2):
+            later.append(lax.ppermute(later[-1], ("span", "blade"), down))
+        line = jnp.concatenate([*earlier[::-1], *later[1:]], axis=1)
+        moment_all = jnp.roll(
+            line, (lax.axis_index(("span", "blade")) - ways // 2) * moment_got.shape[1], axis=1
+        )
         turn_frac = azimuth.astype(jnp.float32) / naz_total
         source_angle = 2.0 * math.pi * (turn_frac + column_frac)
         source_cos = jnp.cos(source_angle)

time: 258 us -> 245 us (0.950)
  blocking collectives: 34.4 us -> 19.3 us
  starting transfers between devices: 77.3 us -> 81.8 us
    all_gather x3 -> x0, blocking collectives: 15.9 us -> none  [on_device(): lax.all_gather(moment_got, ('span', 'blade'), axis=1, tiled=True)]
    ppermute x0 -> x9, starting transfers between devices: none -> 6.08 us  [the longest x3 3.3 us: on_device(): later.append(lax.ppermute(later[-1], ('span', 'blade'), down))]
  transfers between devices with their start and end apart: 27 -> 36, of which waited for: 14 -> 14; matrix products, arithmetic and copies ran while one was open for 15% -> 14% of each run, Pallas kernels for 0% -> 0%
where the time goes in v1:
time: 245 us; the launch traced here: 244 us
  other arithmetic  89.1 us (36%)
  starting transfers between devices  81.8 us (33%)
  waiting for transfers between devices  20.7 us (8%)
  blocking collectives  19.3 us (8%)
  local copies, waits for them, and re-layouts  15.1 us (6%)
  between operations  11.8 us (5%)
  loops' own time  5.87 us (2%)
    ppermute x12, starting transfers between devices, with_halo(): lax.ppermute(tail, axis, [(i, (i + 1) % count) for i in range(ends)])  48.1 us
    ppermute x12, starting transfers between devices, with_halo(): lax.ppermute(head, axis, [((i + 1) % count, i) for i in range(ends)])  15.5 us
    sub x48, other arithmetic, near_velocity(): strengths[1][None, :] * separation[2]  14.4 us
    psum x1, blocking collectives, spread(): return lax.psum(jnp.where(mine, shard, jnp.zeros_like(shard)), axis)  13.9 us
    reduce_sum x48, other arithmetic, far_velocity(): return inv_four_pi * jnp.sum(values, axis=2)  13.4 us
    ppermute x3, starting transfers between devices, shifted(): lax.ppermute(value, axis, [(source, source + steps) for source in range(f...  12.1 us
    ppermute x12, waiting for transfers between devices, with_halo(): lax.ppermute(head, axis, [((i + 1) % count, i) for i in range(ends)])  10.8 us
    reduce_sum x48, other arithmetic, near_velocity(): dist_sq = jnp.sum(separation * separation, axis=0) + near_core  10.6 us
  transfers between devices with their start and end apart: 36, of which 14 were waited for; matrix products, arithmetic and copies ran while one was open for 14% of the time, Pallas kernels for 0%

profile of v1, /device:TPU:0, one launch (start us, length us, event | category | flops | bytes accessed | tf_op | source)
XLA Modules:
  0.0 243.6 jit_solution(17921101156365543727)
XLA Ops:
  14.2 13.9 %all-reduce = (f32[3,128]{1,0:T(4,128)S(1)}, f32[1,2,64]{2,1,0:T(2,128)S(1)}, f32[3,128]{1,0:T(4,128)S(1)}, f32[1,2,64]{2,1,0:T(2,128)S(1)}, f32[3,128]{1,0:T(4,128)S(1)}, /*index=5*/f32[1,2,64]{2,1,0:T(2,128)S(1)}) all-reduce(f32[3,128]{1,0:T(4,128)S(1)} %select_n.386, ...), channel_id=1, replica_groups=mesh['groups'=2,'age'=4,'span'=2,'blade'=2] {'age'}, use_global_device_ids=true, to_apply=%region_5.6 | all-reduce | flops 1536 | bytes 12288 | tf_op jit(solution)/shard_map/psum | solution.py:16
  36.6 5.4 %all_gather.3 = f32[3,512]{1,0:T(4,128)S(1)} all-gather(f32[3,128]{1,0:T(4,128)S(1)} %div.142), channel_id=1, replica_groups=mesh['groups'=2,'age'=4,'span'=2,'blade'=2] {'span','blade'}, dimensions={1}, use_global_device_ids=true | all-gather | bytes 7680 | tf_op jit(solution)/shard_map/all_gather | solution.py:146
  44.3 4.5 %collective-permute-start.5 = (f32[4,2,18,1]{3,1,2,0:T(2,128)S(1)}, f32[4,2,18,1]{3,1,2,0:T(2,128)S(1)}, u32[]{:S(2)}, u32[]{:S(2)}) collective-permute-start(f32[4,2,18,1]{3,1,2,0:T(2,128)S(1)} %get-tuple-element.399), channel_id=1, source_target_pairs={{0,2},{1,3},{4,6},{5,7},{8,10},{9,11},{12,14},{13,15},{16,18},{17,... | collective-permute-start | bytes 1736 | tf_op jit(solution)/shard_map/ppermute | solution.py:27
  53.9 4.9 %collective-permute-start.7 = (f32[2,1,1,8,6,128]{5,3,0,4,2,1:T(8,128)S(1)}, f32[2,1,1,8,6,128]{5,3,0,4,2,1:T(8,128)S(1)}, u32[]{:S(2)}, u32[]{:S(2)}) collective-permute-start(f32[2,1,1,8,6,128]{5,3,0,4,2,1:T(8,128)S(1)} %maximum_bitcast_fusion.3), channel_id=1, source_target_pairs={{0,4},{4,8},{8,12},{1,5},{5,9},{9,13},{2,6},{6,10},{10,14},{3,7},{... | collective-permute-start | bytes 147464 | tf_op jit(solution)/shard_map/ppermute | solution.py:27
  59.0 9.9 %while.60 = (s32[]{:T(128)}, f32[16,1,3,128]{3,2,1,0:T(4,128)S(1)}, f32[3,512]{1,0:T(4,128)S(1)}, f32[16,1,3,128]{3,2,1,0:T(4,128)S(1)}, f32[3,512]{1,0:T(4,128)S(1)}, /*index=5*/s32[]{:T(128)}) while((s32[]{:T(128)}, f32[16,1,3,128]{3,2,1,0:T(4,128)S(1)}, f32[3,512]{1,0:T(4,128)S(1)}, f32[16,1,3,128]{3,2,1,0:T(4,128)S(1)}, ...), condition=%wide.region_10.12_spmd, body=%wide.region_6.11_spmd.sunk | while | flops 2293762 | bytes 2133589 | solution.py:101
  74.2 4.6 %collective-permute-start.9 = (f32[2,3,1,8,6,128]{5,3,0,4,2,1:T(8,128)S(1)}, f32[2,3,1,8,6,128]{5,3,0,4,2,1:T(8,128)S(1)}, u32[]{:S(2)}, u32[]{:S(2)}) collective-permute-start(f32[2,3,1,8,6,128]{5,3,0,4,2,1:T(8,128)S(1)} %pad_maximum_fusion.3), channel_id=1, source_target_pairs={{0,2},{1,3},{4,6},{5,7},{8,10},{9,11},{12,14},{13,15},{16,18},{17,... | collective-permute-start | bytes 442376 | tf_op jit(solution)/shard_map/ppermute | solution.py:27
  83.3 19.9 %while.61 = (s32[]{:T(128)}, f32[16,1,3,128]{3,2,1,0:T(4,128)S(1)}, f32[16,1,3,1024]{3,0,2,1:T(8,128)S(1)}, f32[16,1,3,128]{3,2,1,0:T(4,128)S(1)}, f32[16,1,3,1024]{3,0,2,1:T(8,128)S(1)}, /*index=5*/s32[]{:T(128)}) while((s32[]{:T(128)}, f32[16,1,3,128]{3,2,1,0:T(4,128)S(1)}, f32[16,1,3,1024]{3,0,2,1:T(8,128)S(1)}, ...), condition=%wide.region_14.16_spmd, body=%wide.region_11.15_spmd.sunk | while | flops 4587522 | bytes 8560217 | solution.py:101
  103.5 3.6 %collective-permute-start.11 = (f32[4,2,64]{2,1,0:T(2,128)S(1)}, f32[4,2,64]{2,1,0:T(2,128)S(1)}, u32[]{:S(2)}, u32[]{:S(2)}) collective-permute-start(f32[4,2,64]{2,1,0:T(2,128)S(1)} %get-tuple-element.404), channel_id=1, source_target_pairs={{0,4},{4,8},{8,12},{1,5},{5,9},{9,13},{2,6},{6,10},{10,14},{3,7},{... | collective-permute-start | bytes 6152 | tf_op jit(solution)/shard_map/ppermute | solution.py:39
  107.3 2.5 %collective-permute-start.15 = (f32[4,2,1,64]{3,1,0,2:T(2,128)S(1)}, f32[4,2,1,64]{3,1,0,2:T(2,128)S(1)}, u32[]{:S(2)}, u32[]{:S(2)}) collective-permute-start(f32[4,2,1,64]{3,1,0,2:T(2,128)S(1)} %get-tuple-element.403), channel_id=1, source_target_pairs={{0,4},{4,8},{8,12},{1,5},{5,9},{9,13},{2,6},{6,10},{10,14},{3,7},{... | collective-permute-start | bytes 6152 | tf_op jit(solution)/shard_map/ppermute | solution.py:27
  111.1 4.1 %collective-permute-done.16 = f32[4,2,1,64]{3,1,0,2:T(2,128)S(1)} collective-permute-done((f32[4,2,1,64]{3,1,0,2:T(2,128)S(1)}, f32[4,2,1,64]{3,1,0,2:T(2,128)S(1)}, u32[]{:S(2)}, u32[]{:S(2)}) %collective-permute-start.16) | collective-permute-done | bytes 2080 | tf_op jit(solution)/shard_map/ppermute | solution.py:29
  116.8 4.5 %collective-permute-start.17 = (f32[4,2,18,1]{3,1,0,2:T(2,128)S(1)}, f32[4,2,18,1]{3,1,0,2:T(2,128)S(1)}, u32[]{:S(2)}, u32[]{:S(2)}) collective-permute-start(f32[4,2,18,1]{3,1,0,2:T(2,128)S(1)} %get-tuple-element.397), channel_id=1, source_target_pairs={{0,2},{1,3},{4,6},{5,7},{8,10},{9,11},{12,14},{13,15},{16,18},{17,... | collective-permute-start | bytes 1736 | tf_op jit(solution)/shard_map/ppermute | solution.py:27
  126.0 4.5 %collective-permute-start.19 = (f32[2,1,1,8,6,128]{5,3,0,4,2,1:T(8,128)S(1)}, f32[2,1,1,8,6,128]{5,3,0,4,2,1:T(8,128)S(1)}, u32[]{:S(2)}, u32[]{:S(2)}) collective-permute-start(f32[2,1,1,8,6,128]{5,3,0,4,2,1:T(8,128)S(1)} %maximum_bitcast_fusion.4), channel_id=1, source_target_pairs={{0,4},{4,8},{8,12},{1,5},{5,9},{9,13},{2,6},{6,10},{10,14},{3,7},{... | collective-permute-start | bytes 147464 | tf_op jit(solution)/shard_map/ppermute | solution.py:27
  133.6 4.7 %collective-permute-start.21 = (f32[2,3,1,8,6,128]{5,3,0,4,2,1:T(8,128)S(1)}, f32[2,3,1,8,6,128]{5,3,0,4,2,1:T(8,128)S(1)}, u32[]{:S(2)}, u32[]{:S(2)}) collective-permute-start(f32[2,3,1,8,6,128]{5,3,0,4,2,1:T(8,128)S(1)} %pad_maximum_fusion.4), channel_id=1, source_target_pairs={{0,2},{1,3},{4,6},{5,7},{8,10},{9,11},{12,14},{13,15},{16,18},{17,... | collective-permute-start | bytes 442376 | tf_op jit(solution)/shard_map/ppermute | solution.py:27
  138.4 9.9 %while.62 = (s32[]{:T(128)}, f32[16,1,3,128]{3,2,1,0:T(4,128)S(1)}, f32[3,512]{1,0:T(4,128)S(1)}, f32[16,1,3,128]{3,2,1,0:T(4,128)S(1)}, f32[3,512]{1,0:T(4,128)S(1)}, /*index=5*/s32[]{:T(128)}) while((s32[]{:T(128)}, f32[16,1,3,128]{3,2,1,0:T(4,128)S(1)}, f32[3,512]{1,0:T(4,128)S(1)}, f32[16,1,3,128]{3,2,1,0:T(4,128)S(1)}, ...), condition=%wide.region_21.23_spmd, body=%wide.region_17.22_spmd.sunk | while | flops 2293762 | bytes 2133589 | solution.py:101
  149.9 19.9 %while.63 = (s32[]{:T(128)}, f32[16,1,3,128]{3,2,1,0:T(4,128)S(1)}, f32[16,1,3,1024]{3,0,2,1:T(8,128)S(1)}, f32[16,1,3,128]{3,2,1,0:T(4,128)S(1)}, f32[16,1,3,1024]{3,0,2,1:T(8,128)S(1)}, /*index=5*/s32[]{:T(128)}) while((s32[]{:T(128)}, f32[16,1,3,128]{3,2,1,0:T(4,128)S(1)}, f32[16,1,3,1024]{3,0,2,1:T(8,128)S(1)}, ...), condition=%wide.region_25.27_spmd, body=%wide.region_22.26_spmd.sunk | while | flops 4587522 | bytes 8560217 | solution.py:101
  170.1 4.2 %collective-permute-start.23 = (f32[4,2,64]{2,1,0:T(2,128)S(1)}, f32[4,2,64]{2,1,0:T(2,128)S(1)}, u32[]{:S(2)}, u32[]{:S(2)}) collective-permute-start(f32[4,2,64]{2,1,0:T(2,128)S(1)} %get-tuple-element.402), channel_id=1, source_target_pairs={{0,4},{4,8},{8,12},{1,5},{5,9},{9,13},{2,6},{6,10},{10,14},{3,7},{... | collective-permute-start | bytes 6152 | tf_op jit(solution)/shard_map/ppermute | solution.py:39
  174.4 2.8 %collective-permute-start.27 = (f32[4,2,1,64]{3,1,0,2:T(2,128)S(1)}, f32[4,2,1,64]{3,1,0,2:T(2,128)S(1)}, u32[]{:S(2)}, u32[]{:S(2)}) collective-permute-start(f32[4,2,1,64]{3,1,0,2:T(2,128)S(1)} %get-tuple-element.401), channel_id=1, source_target_pairs={{0,4},{4,8},{8,12},{1,5},{5,9},{9,13},{2,6},{6,10},{10,14},{3,7},{... | collective-permute-start | bytes 6152 | tf_op jit(solution)/shard_map/ppermute | solution.py:27
  178.6 4.2 %collective-permute-done.28 = f32[4,2,1,64]{3,1,2,0:T(2,128)S(1)} collective-permute-done((f32[4,2,1,64]{3,1,2,0:T(2,128)S(1)}, f32[4,2,1,64]{3,1,2,0:T(2,128)S(1)}, u32[]{:S(2)}, u32[]{:S(2)}) %collective-permute-start.28) | collective-permute-done | bytes 2080 | tf_op jit(solution)/shard_map/ppermute | solution.py:29
  184.2 4.5 %collective-permute-start.29 = (f32[4,2,18,1]{3,1,2,0:T(2,128)S(1)}, f32[4,2,18,1]{3,1,2,0:T(2,128)S(1)}, u32[]{:S(2)}, u32[]{:S(2)}) collective-permute-start(f32[4,2,18,1]{3,1,2,0:T(2,128)S(1)} %get-tuple-element.395), channel_id=1, source_target_pairs={{0,2},{1,3},{4,6},{5,7},{8,10},{9,11},{12,14},{13,15},{16,18},{17,... | collective-permute-start | bytes 1736 | tf_op jit(solution)/shard_map/ppermute | solution.py:27
  193.5 4.5 %collective-permute-start.31 = (f32[2,1,1,8,6,128]{5,3,0,4,2,1:T(8,128)S(1)}, f32[2,1,1,8,6,128]{5,3,0,4,2,1:T(8,128)S(1)}, u32[]{:S(2)}, u32[]{:S(2)}) collective-permute-start(f32[2,1,1,8,6,128]{5,3,0,4,2,1:T(8,128)S(1)} %maximum_bitcast_fusion.5), channel_id=1, source_target_pairs={{0,4},{4,8},{8,12},{1,5},{5,9},{9,13},{2,6},{6,10},{10,14},{3,7},{... | collective-permute-start | bytes 147464 | tf_op jit(solution)/shard_map/ppermute | solution.py:27
  201.1 4.6 %collective-permute-start.33 = (f32[2,3,1,8,6,128]{5,3,0,4,2,1:T(8,128)S(1)}, f32[2,3,1,8,6,128]{5,3,0,4,2,1:T(8,128)S(1)}, u32[]{:S(2)}, u32[]{:S(2)}) collective-permute-start(f32[2,3,1,8,6,128]{5,3,0,4,2,1:T(8,128)S(1)} %pad_maximum_fusion.5), channel_id=1, source_target_pairs={{0,2},{1,3},{4,6},{5,7},{8,10},{9,11},{12,14},{13,15},{16,18},{17,... | collective-permute-start | bytes 442376 | tf_op jit(solution)/shard_map/ppermute | solution.py:27
  205.7 9.9 %while.64 = (s32[]{:T(128)}, f32[16,1,3,128]{3,2,1,0:T(4,128)S(1)}, f32[3,512]{1,0:T(4,128)S(1)}, f32[16,1,3,128]{3,2,1,0:T(4,128)S(1)}, f32[3,512]{1,0:T(4,128)S(1)}, /*index=5*/s32[]{:T(128)}) while((s32[]{:T(128)}, f32[16,1,3,128]{3,2,1,0:T(4,128)S(1)}, f32[3,512]{1,0:T(4,128)S(1)}, f32[16,1,3,128]{3,2,1,0:T(4,128)S(1)}, ...), condition=%wide.region_32.34_spmd, body=%wide.region_28.33_spmd.sunk | while | flops 2293762 | bytes 2133589 | solution.py:101
  217.2 19.9 %while.65 = (s32[]{:T(128)}, f32[16,1,3,128]{3,2,1,0:T(4,128)S(1)}, f32[16,1,3,1024]{3,0,2,1:T(8,128)S(1)}, f32[16,1,3,128]{3,2,1,0:T(4,128)S(1)}, f32[16,1,3,1024]{3,0,2,1:T(8,128)S(1)}, /*index=5*/s32[]{:T(128)}) while((s32[]{:T(128)}, f32[16,1,3,128]{3,2,1,0:T(4,128)S(1)}, f32[16,1,3,1024]{3,0,2,1:T(8,128)S(1)}, ...), condition=%wide.region_36.38_spmd, body=%wide.region_33.37_spmd.sunk | while | flops 4587522 | bytes 8560217 | solution.py:101
  237.3 4.2 %collective-permute-start.35 = (f32[4,2,64]{2,1,0:T(2,128)S(1)}, f32[4,2,64]{2,1,0:T(2,128)S(1)}, u32[]{:S(2)}, u32[]{:S(2)}) collective-permute-start(f32[4,2,64]{2,1,0:T(2,128)S(1)} %bitcast.385), channel_id=1, source_target_pairs={{0,4},{4,8},{8,12},{1,5},{5,9},{9,13},{2,6},{6,10},{10,14},{3,7},{... | collective-permute-start | bytes 6152 | tf_op jit(solution)/shard_map/ppermute | solution.py:39
  (1002 shorter events, 139.4 us)
Async XLA Ops:
  28.1 20.8 %collective-permute-start = (f32[3,128]{1,0:T(4,128)S(1)}, f32[3,128]{1,0:T(4,128)S(1)}, u32[]{:S(2)}, u32[]{:S(2)}) collective-permute-start(f32[3,128]{1,0:T(4,128)S(1)} %get-tuple-element.345), channel_id=1, source_target_pairs={{0,1},{1,2},{2,3},{3,0},{4,5},{5,6},{6,7},{7,4},{8,9},{9,10},{10,1... | collective-permute-start | bytes 4616 | tf_op jit(solution)/shard_map/ppermute | solution.py:166
  28.1 24.1 %collective-permute-start.2 = (f32[3,128]{1,0:T(4,128)S(1)}, f32[3,128]{1,0:T(4,128)S(1)}, u32[]{:S(2)}, u32[]{:S(2)}) collective-permute-start(f32[3,128]{1,0:T(4,128)S(1)} %get-tuple-element.345), channel_id=1, source_target_pairs={{0,3},{1,0},{2,1},{3,2},{4,7},{5,4},{6,5},{7,6},{8,11},{9,8},{10,9... | collective-permute-start | bytes 4616 | tf_op jit(solution)/shard_map/ppermute | solution.py:168
  31.2 11.6 %collective-permute-start.3 = (f32[4,2,1,64]{3,1,2,0:T(2,128)S(1)}, f32[4,2,1,64]{3,1,2,0:T(2,128)S(1)}, u32[]{:S(2)}, u32[]{:S(2)}) collective-permute-start(f32[4,2,1,64]{3,1,2,0:T(2,128)S(1)} %copy.303), channel_id=1, source_target_pairs={{0,4},{4,8},{8,12},{1,5},{5,9},{9,13},{2,6},{6,10},{10,14},{3,7},{... | collective-permute-start | bytes 6152 | tf_op jit(solution)/shard_map/ppermute | solution.py:27
  32.5 10.3 %collective-permute-start.4 = (f32[4,2,1,64]{3,1,2,0:T(2,128)S(1)}, f32[4,2,1,64]{3,1,2,0:T(2,128)S(1)}, u32[]{:S(2)}, u32[]{:S(2)}) collective-permute-start(f32[4,2,1,64]{3,1,2,0:T(2,128)S(1)} %copy.304), channel_id=1, source_target_pairs={{4,0},{8,4},{12,8},{5,1},{9,5},{13,9},{6,2},{10,6},{14,10},{7,3},{... | collective-permute-start | bytes 6152 | tf_op jit(solution)/shard_map/ppermute | solution.py:29
  33.8 35.0 %collective-permute-start.24 = (f32[3,128]{1,0:T(4,128)S(1)}, f32[3,128]{1,0:T(4,128)S(1)}, u32[]{:S(2)}, u32[]{:S(2)}) collective-permute-start(f32[3,128]{1,0:T(4,128)S(1)} %get-tuple-element.349), channel_id=1, source_target_pairs={{0,1},{1,2},{2,3},{3,0},{4,5},{5,6},{6,7},{7,4},{8,9},{9,10},{10,1... | collective-permute-start | bytes 4616 | tf_op jit(solution)/shard_map/ppermute | solution.py:166
  44.3 6.5 %collective-permute-start.5 = (f32[4,2,18,1]{3,1,2,0:T(2,128)S(1)}, f32[4,2,18,1]{3,1,2,0:T(2,128)S(1)}, u32[]{:S(2)}, u32[]{:S(2)}) collective-permute-start(f32[4,2,18,1]{3,1,2,0:T(2,128)S(1)} %get-tuple-element.399), channel_id=1, source_target_pairs={{0,2},{1,3},{4,6},{5,7},{8,10},{9,11},{12,14},{13,15},{16,18},{17,... | collective-permute-start | bytes 1736 | tf_op jit(solution)/shard_map/ppermute | solution.py:27
  48.9 25.3 %collective-permute-start.26 = (f32[3,128]{1,0:T(4,128)S(1)}, f32[3,128]{1,0:T(4,128)S(1)}, u32[]{:S(2)}, u32[]{:S(2)}) collective-permute-start(f32[3,128]{1,0:T(4,128)S(1)} %get-tuple-element.349), channel_id=1, source_target_pairs={{0,3},{1,0},{2,1},{3,2},{4,7},{5,4},{6,5},{7,6},{8,11},{9,8},{10,9... | collective-permute-start | bytes 4616 | tf_op jit(solution)/shard_map/ppermute | solution.py:168
  49.3 21.1 %collective-permute-start.12 = (f32[3,128]{1,0:T(4,128)S(1)}, f32[3,128]{1,0:T(4,128)S(1)}, u32[]{:S(2)}, u32[]{:S(2)}) collective-permute-start(f32[3,128]{1,0:T(4,128)S(1)} %get-tuple-element.347), channel_id=1, source_target_pairs={{0,1},{1,2},{2,3},{3,0},{4,5},{5,6},{6,7},{7,4},{8,9},{9,10},{10,1... | collective-permute-start | bytes 4616 | tf_op jit(solution)/shard_map/ppermute | solution.py:166
  52.3 18.9 %collective-permute-start.8 = (f32[2,1,1,8,6,128]{5,3,0,4,2,1:T(8,128)S(1)}, f32[2,1,1,8,6,128]{5,3,0,4,2,1:T(8,128)S(1)}, u32[]{:S(2)}, u32[]{:S(2)}) collective-permute-start(f32[2,1,1,8,6,128]{5,3,0,4,2,1:T(8,128)S(1)} %maximum_bitcast_fusion.3), channel_id=1, source_target_pairs={{4,0},{8,4},{12,8},{5,1},{9,5},{13,9},{6,2},{10,6},{14,10},{7,3},{... | collective-permute-start | bytes 147464 | tf_op jit(solution)/shard_map/ppermute | solution.py:29
  53.9 19.0 %collective-permute-start.7 = (f32[2,1,1,8,6,128]{5,3,0,4,2,1:T(8,128)S(1)}, f32[2,1,1,8,6,128]{5,3,0,4,2,1:T(8,128)S(1)}, u32[]{:S(2)}, u32[]{:S(2)}) collective-permute-start(f32[2,1,1,8,6,128]{5,3,0,4,2,1:T(8,128)S(1)} %maximum_bitcast_fusion.3), channel_id=1, source_target_pairs={{0,4},{4,8},{8,12},{1,5},{5,9},{9,13},{2,6},{6,10},{10,14},{3,7},{... | collective-permute-start | bytes 147464 | tf_op jit(solution)/shard_map/ppermute | solution.py:27
  68.9 10.1 %collective-permute-start.14 = (f32[3,128]{1,0:T(4,128)S(1)}, f32[3,128]{1,0:T(4,128)S(1)}, u32[]{:S(2)}, u32[]{:S(2)}) collective-permute-start(f32[3,128]{1,0:T(4,128)S(1)} %get-tuple-element.347), channel_id=1, source_target_pairs={{0,3},{1,0},{2,1},{3,2},{4,7},{5,4},{6,5},{7,6},{8,11},{9,8},{10,9... | collective-permute-start | bytes 4616 | tf_op jit(solution)/shard_map/ppermute | solution.py:168
  70.4 8.4 %collective-permute-start.25 = (f32[3,128]{1,0:T(4,128)S(1)}, f32[3,128]{1,0:T(4,128)S(1)}, u32[]{:S(2)}, u32[]{:S(2)}) collective-permute-start(f32[3,128]{1,0:T(4,128)S(1)} %collective-permute-done.24), channel_id=1, source_target_pairs={{0,1},{1,2},{2,3},{3,0},{4,5},{5,6},{6,7},{7,4},{8,9},{9,10},{10,1... | collective-permute-start | bytes 4616 | tf_op jit(solution)/shard_map/ppermute | solution.py:166
  71.2 7.7 %collective-permute-start.13 = (f32[3,128]{1,0:T(4,128)S(1)}, f32[3,128]{1,0:T(4,128)S(1)}, u32[]{:S(2)}, u32[]{:S(2)}) collective-permute-start(f32[3,128]{1,0:T(4,128)S(1)} %collective-permute-done.12), channel_id=1, source_target_pairs={{0,1},{1,2},{2,3},{3,0},{4,5},{5,6},{6,7},{7,4},{8,9},{9,10},{10,1... | collective-permute-start | bytes 4616 | tf_op jit(solution)/shard_map/ppermute | solution.py:166
  72.9 7.7 %collective-permute-start.10 = (f32[2,3,1,8,6,128]{5,3,0,4,2,1:T(8,128)S(1)}, f32[2,3,1,8,6,128]{5,3,0,4,2,1:T(8,128)S(1)}, u32[]{:S(2)}, u32[]{:S(2)}) collective-permute-start(f32[2,3,1,8,6,128]{5,3,0,4,2,1:T(8,128)S(1)} %pad_maximum_fusion.3), channel_id=1, source_target_pairs={{2,0},{3,1},{6,4},{7,5},{10,8},{11,9},{14,12},{15,13},{18,16},{19,... | collective-permute-start | bytes 442376 | tf_op jit(solution)/shard_map/ppermute | solution.py:29
  74.2 7.6 %collective-permute-start.9 = (f32[2,3,1,8,6,128]{5,3,0,4,2,1:T(8,128)S(1)}, f32[2,3,1,8,6,128]{5,3,0,4,2,1:T(8,128)S(1)}, u32[]{:S(2)}, u32[]{:S(2)}) collective-permute-start(f32[2,3,1,8,6,128]{5,3,0,4,2,1:T(8,128)S(1)} %pad_maximum_fusion.3), channel_id=1, source_target_pairs={{0,2},{1,3},{4,6},{5,7},{8,10},{9,11},{12,14},{13,15},{16,18},{17,... | collective-permute-start | bytes 442376 | tf_op jit(solution)/shard_map/ppermute | solution.py:27
  116.8 6.5 %collective-permute-start.17 = (f32[4,2,18,1]{3,1,0,2:T(2,128)S(1)}, f32[4,2,18,1]{3,1,0,2:T(2,128)S(1)}, u32[]{:S(2)}, u32[]{:S(2)}) collective-permute-start(f32[4,2,18,1]{3,1,0,2:T(2,128)S(1)} %get-tuple-element.397), channel_id=1, source_target_pairs={{0,2},{1,3},{4,6},{5,7},{8,10},{9,11},{12,14},{13,15},{16,18},{17,... | collective-permute-start | bytes 1736 | tf_op jit(solution)/shard_map/ppermute | solution.py:27
  126.0 6.3 %collective-permute-start.19 = (f32[2,1,1,8,6,128]{5,3,0,4,2,1:T(8,128)S(1)}, f32[2,1,1,8,6,128]{5,3,0,4,2,1:T(8,128)S(1)}, u32[]{:S(2)}, u32[]{:S(2)}) collective-permute-start(f32[2,1,1,8,6,128]{5,3,0,4,2,1:T(8,128)S(1)} %maximum_bitcast_fusion.4), channel_id=1, source_target_pairs={{0,4},{4,8},{8,12},{1,5},{5,9},{9,13},{2,6},{6,10},{10,14},{3,7},{... | collective-permute-start | bytes 147464 | tf_op jit(solution)/shard_map/ppermute | solution.py:27
  132.3 16.1 %collective-permute-start.22 = (f32[2,3,1,8,6,128]{5,3,0,4,2,1:T(8,128)S(1)}, f32[2,3,1,8,6,128]{5,3,0,4,2,1:T(8,128)S(1)}, u32[]{:S(2)}, u32[]{:S(2)}) collective-permute-start(f32[2,3,1,8,6,128]{5,3,0,4,2,1:T(8,128)S(1)} %pad_maximum_fusion.4), channel_id=1, source_target_pairs={{2,0},{3,1},{6,4},{7,5},{10,8},{11,9},{14,12},{15,13},{18,16},{19,... | collective-permute-start | bytes 442376 | tf_op jit(solution)/shard_map/ppermute | solution.py:29
  133.6 14.8 %collective-permute-start.21 = (f32[2,3,1,8,6,128]{5,3,0,4,2,1:T(8,128)S(1)}, f32[2,3,1,8,6,128]{5,3,0,4,2,1:T(8,128)S(1)}, u32[]{:S(2)}, u32[]{:S(2)}) collective-permute-start(f32[2,3,1,8,6,128]{5,3,0,4,2,1:T(8,128)S(1)} %pad_maximum_fusion.4), channel_id=1, source_target_pairs={{0,2},{1,3},{4,6},{5,7},{8,10},{9,11},{12,14},{13,15},{16,18},{17,... | collective-permute-start | bytes 442376 | tf_op jit(solution)/shard_map/ppermute | solution.py:27
  170.1 7.1 %collective-permute-start.23 = (f32[4,2,64]{2,1,0:T(2,128)S(1)}, f32[4,2,64]{2,1,0:T(2,128)S(1)}, u32[]{:S(2)}, u32[]{:S(2)}) collective-permute-start(f32[4,2,64]{2,1,0:T(2,128)S(1)} %get-tuple-element.402), channel_id=1, source_target_pairs={{0,4},{4,8},{8,12},{1,5},{5,9},{9,13},{2,6},{6,10},{10,14},{3,7},{... | collective-permute-start | bytes 6152 | tf_op jit(solution)/shard_map/ppermute | solution.py:39
  184.2 6.5 %collective-permute-start.29 = (f32[4,2,18,1]{3,1,2,0:T(2,128)S(1)}, f32[4,2,18,1]{3,1,2,0:T(2,128)S(1)}, u32[]{:S(2)}, u32[]{:S(2)}) collective-permute-start(f32[4,2,18,1]{3,1,2,0:T(2,128)S(1)} %get-tuple-element.395), channel_id=1, source_target_pairs={{0,2},{1,3},{4,6},{5,7},{8,10},{9,11},{12,14},{13,15},{16,18},{17,... | collective-permute-start | bytes 1736 | tf_op jit(solution)/shard_map/ppermute | solution.py:27
  193.5 6.3 %collective-permute-start.31 = (f32[2,1,1,8,6,128]{5,3,0,4,2,1:T(8,128)S(1)}, f32[2,1,1,8,6,128]{5,3,0,4,2,1:T(8,128)S(1)}, u32[]{:S(2)}, u32[]{:S(2)}) collective-permute-start(f32[2,1,1,8,6,128]{5,3,0,4,2,1:T(8,128)S(1)} %maximum_bitcast_fusion.5), channel_id=1, source_target_pairs={{0,4},{4,8},{8,12},{1,5},{5,9},{9,13},{2,6},{6,10},{10,14},{3,7},{... | collective-permute-start | bytes 147464 | tf_op jit(solution)/shard_map/ppermute | solution.py:27
  199.8 15.9 %collective-permute-start.34 = (f32[2,3,1,8,6,128]{5,3,0,4,2,1:T(8,128)S(1)}, f32[2,3,1,8,6,128]{5,3,0,4,2,1:T(8,128)S(1)}, u32[]{:S(2)}, u32[]{:S(2)}) collective-permute-start(f32[2,3,1,8,6,128]{5,3,0,4,2,1:T(8,128)S(1)} %pad_maximum_fusion.5), channel_id=1, source_target_pairs={{2,0},{3,1},{6,4},{7,5},{10,8},{11,9},{14,12},{15,13},{18,16},{19,... | collective-permute-start | bytes 442376 | tf_op jit(solution)/shard_map/ppermute | solution.py:29
  201.1 14.6 %collective-permute-start.33 = (f32[2,3,1,8,6,128]{5,3,0,4,2,1:T(8,128)S(1)}, f32[2,3,1,8,6,128]{5,3,0,4,2,1:T(8,128)S(1)}, u32[]{:S(2)}, u32[]{:S(2)}) collective-permute-start(f32[2,3,1,8,6,128]{5,3,0,4,2,1:T(8,128)S(1)} %pad_maximum_fusion.5), channel_id=1, source_target_pairs={{0,2},{1,3},{4,6},{5,7},{8,10},{9,11},{12,14},{13,15},{16,18},{17,... | collective-permute-start | bytes 442376 | tf_op jit(solution)/shard_map/ppermute | solution.py:27
  (17 other events, 151.2 us)
